TPU v7x, 32 devices: a whole 2x2x4 slice. The times are simulated.
32 devices in a mesh: row: 4 (over x, core), col: 8 (over z, y).
Axes of the slice: x: 2, y: 2, z: 4, core: 2. Of those that a mesh axis runs over, the one named last changes fastest.
Arguments:
- gradient: bfloat16 [4352, 8192], P('row', 'col'), may hold values from -0.03125 to 0.03125
Outputs:
- update: bfloat16 [4352, 8192], P('row', 'col')
All inputs are finite; a program needn't handle non-finite values.
Results may differ from a plain program's by a relative error of at most 0.0048.
Values may be sent and summed in bfloat16 or wider, within the bound.
No kernel may reach another device: no remote copies, remote signals or barrier semaphores. Data moves between devices by JAX's collectives and lax.ppermute only.
A program may use at most 128 MiB of HBM per device.

v0:
```python
import math

import jax
import jax.numpy as jnp
from jax import lax
from jax.sharding import PartitionSpec as P

N = 8192


A_COEF = 3.4445
B_COEF = -4.775
C_COEF = 2.0315


def spread(value, axis, source):
    kept = jnp.where(lax.axis_index(axis) == source, value, 0).astype(value.dtype)
    return lax.psum(kept, axis)


def shards(gradient):
    tile_rows = gradient.shape[0]
    row_count = lax.axis_size("row")
    col_count = lax.axis_size("col")
    col_per_row = col_count // row_count
    col_index = lax.axis_index("col")
    gram_width = tile_rows * row_count // col_count
    root_row = col_index // col_per_row
    offset = col_index % col_per_row * gram_width
    contract = (((1,), (1,)), ((), ()))
    column_panel = lax.all_gather(gradient, "row", axis=0, tiled=True)
    row_panel = lax.all_gather(gradient, "col", axis=1, tiled=True)
    picked = lax.dynamic_slice_in_dim(row_panel, offset, gram_width, 0)
    mirror = spread(picked, "row", root_row)
    gram_tile = lax.dot_general(row_panel, mirror, contract, preferred_element_type=jnp.float32)
    gram_tile = gram_tile.astype(jnp.bfloat16)
    gram_panel = lax.all_gather(gram_tile, "col", axis=1, tiled=True)
    gram_columns = lax.all_gather(gram_tile, "row", axis=0, tiled=True)
    square = jnp.dot(gram_panel, gram_columns, preferred_element_type=jnp.float32)
    poly_tile = (B_COEF * gram_tile.astype(jnp.float32) + C_COEF * square).astype(jnp.bfloat16)
    product = jnp.dot(
        lax.all_gather(poly_tile, "col", axis=1, tiled=True),
        column_panel,
        preferred_element_type=jnp.float32,
    )
    rms_scale = math.sqrt(N)
    return (rms_scale * (A_COEF * gradient.astype(jnp.float32) + product)).astype(jnp.bfloat16)


def solution(mesh):
    in_specs = (P("row", "col"),)
    out_specs = P("row", "col")
    return jax.shard_map(shards, mesh=mesh, in_specs=in_specs, out_specs=out_specs, check_vma=False)
```

profile of v0, /device:TPU:0, one launch (start us, length us, event | category | flops | bytes accessed | tf_op | source)
XLA Modules:
  0.0 961.5 jit_solution(94495843375195053)
XLA Ops:
  6.5 0.0 all-gather.7.cloned.1.call-start
  6.5 0.7 all-gather.7.cloned.1.call-update
  7.3 0.0 all-reduce.2.cloned.1.call-start
  7.3 347.1 %all-gather.7.cloned.1.call-done = bf16[1088,8192]{1,0:T(8,128)(2,1)} async-done(((bf16[1088,1024]{1,0:T(8,128)(2,1)}), bf16[1088,8192]{1,0:T(8,128)(2,1)}) %all-gather.7.cloned.1.call-update) | async-done | bytes 17825808 | tf_op jit(solution)/shard_map/all_gather | solution.py:32
  354.4 9.2 dynamic-slice_select_fusion
  363.6 0.0 all-reduce.2.cloned.1.call-update
  363.7 0.0 all-gather.15.cloned.1.call-start
  363.7 161.4 %all-reduce.2.cloned.1.call-done = bf16[544,8192]{1,0:T(8,128)(2,1)} async-done(((bf16[544,8192]{1,0:T(8,128)(2,1)}), bf16[544,8192]{1,0:T(8,128)(2,1)}) %all-reduce.2.cloned.1.call-update) | async-done | bytes 8912912 | tf_op jit(solution)/shard_map/psum | solution.py:18
  525.1 17.9 %convolution_convert_fusion = bf16[544,1088]{1,0:T(8,128)(2,1)} fusion(bf16[544,8192]{1,0:T(8,128)(2,1)} %all-reduce.2.cloned.1.call-done, bf16[1088,8192]{1,0:T(8,128)(2,1)} %all-gather.7.cloned.1.call-done), kind=kOutput, calls=%fused_computation.7 | convolution fusion | flops 9697822720 | bytes 27922432 | tf_op jit(solution)/shard_map/dot_general | solution.py:35
  543.1 0.0 all-gather.15.cloned.1.call-update
  543.1 0.0 all-gather.9.cloned.1.call-start
  543.2 0.5 all-gather.9.cloned.1.call-update
  543.7 0.0 all-gather.13.cloned.1.call-start
  543.7 0.5 all-gather.13.cloned.1.call-update
  544.3 0.2 all-gather.11.cloned.1.call-start
  544.5 38.1 %all-gather.15.cloned.1.call-done = bf16[4,1088,544]{1,2,0:T(8,128)(2,1)} async-done(((bf16[1,1088,544]{1,2,0:T(8,128)(2,1)}), bf16[4,1088,544]{1,2,0:T(8,128)(2,1)}) %all-gather.15.cloned.1.call-update) | async-done | bytes 4734992 | tf_op jit(solution)/shard_map/all_gather | solution.py:38
  582.6 7.2 copy.3
  589.8 9.8 %reshape.1 = bf16[4352,544]{0,1:T(8,128)(2,1)} reshape(bf16[4,1088,544]{1,0,2:T(4,128)(2,1)} %copy.3) | data formatting | bytes 9469952
  599.6 130.3 %all-gather.9.cloned.1.call-done = bf16[1088,4352]{0,1:T(8,128)(2,1)} async-done(((bf16[1088,544]{0,1:T(8,128)(2,1)}), bf16[1088,4352]{0,1:T(8,128)(2,1)}) %all-gather.9.cloned.1.call-update) | async-done | bytes 9469968 | tf_op jit(solution)/shard_map/all_gather | solution.py:37
  729.9 11.9 %fusion.3 = bf16[1088,544]{0,1:T(8,128)(2,1)} fusion(bf16[4352,544]{0,1:T(8,128)(2,1)} %reshape.1, bf16[1088,4352]{0,1:T(8,128)(2,1)} %all-gather.9.cloned.1.call-done, bf16[544,1088]{1,0:T(8,128)(2,1)S(1)} %copy-done.1), kind=kOutput, calls=%fused_computation.6 | convolution fusion | flops 5154613248 | bytes 16572416 | tf_op jit(solution)/shard_map/dot_general | solution.py:39
  741.8 0.0 all-gather.11.cloned.1.call-update
  741.8 49.0 %all-gather.13.cloned.1.call-done = bf16[4352,1024]{1,0:T(8,128)(2,1)} async-done(((bf16[1088,1024]{1,0:T(8,128)(2,1)}), bf16[4352,1024]{1,0:T(8,128)(2,1)}) %all-gather.13.cloned.1.call-update) | async-done | bytes 8912912 | tf_op jit(solution)/shard_map/all_gather | solution.py:31
  790.8 147.3 %all-gather.11.cloned.1.call-done = bf16[1088,4352]{0,1:T(8,128)(2,1)} async-done(((bf16[1088,544]{0,1:T(8,128)(2,1)}), bf16[1088,4352]{0,1:T(8,128)(2,1)}) %all-gather.11.cloned.1.call-update) | async-done | bytes 9469968 | tf_op jit(solution)/shard_map/all_gather | solution.py:42
  938.1 16.6 %fusion.1 = bf16[1088,1024]{1,0:T(8,128)(2,1)} fusion(bf16[1088,4352]{0,1:T(8,128)(2,1)} %all-gather.11.cloned.1.call-done, bf16[4352,1024]{1,0:T(8,128)(2,1)} %all-gather.13.cloned.1.call-done, bf16[1088,1024]{1,0:T(8,128)(2,1)S(1)} %copy-done), kind=kOutput, calls=%fused_computation.3 | convolution fusion | flops 9702801408 | bytes 22839296 | tf_op jit(solution)/shard_map/dot_general | solution.py:41
  (4 shorter events, 0.0 us)
Async XLA Ops:
  6.5 347.9 %all-gather.7.cloned.1.call-start = ((), (), s32[]{:S(2)}) async-start(), calls=%async_computation | async-start | bytes 20054016 | tf_op jit(solution)/shard_map/all_gather | solution.py:32
  7.3 517.9 %all-reduce.2.cloned.1.call-start = ((), (), s32[]{:S(2)}) async-start(), calls=%async_computation.1 | async-start | bytes 17825792 | tf_op jit(solution)/shard_map/psum | solution.py:18
  363.7 218.9 %all-gather.15.cloned.1.call-start = ((), (), s32[]{:S(2)}) async-start(), calls=%async_computation.5 | async-start | bytes 6266880 | tf_op jit(solution)/shard_map/all_gather | solution.py:38
  543.1 186.8 %all-gather.9.cloned.1.call-start = ((), (), s32[]{:S(2)}) async-start(), calls=%async_computation.2 | async-start | bytes 11280384 | tf_op jit(solution)/shard_map/all_gather | solution.py:37
  543.7 247.1 %all-gather.13.cloned.1.call-start = ((), (), s32[]{:S(2)}) async-start(), calls=%async_computation.4 | async-start | bytes 11141120 | tf_op jit(solution)/shard_map/all_gather | solution.py:31
  544.3 393.8 %all-gather.11.cloned.1.call-start = ((), (), s32[]{:S(2)}) async-start(), calls=%async_computation.3 | async-start | bytes 11280384 | tf_op jit(solution)/shard_map/all_gather | solution.py:42
  589.8 140.1 %copy-start.1 = (bf16[544,1088]{1,0:T(8,128)(2,1)S(1)}, bf16[544,1088]{1,0:T(8,128)(2,1)}, u32[]{:S(2)}) copy-start(bf16[544,1088]{1,0:T(8,128)(2,1)} %convolution_convert_fusion) | copy-start | bytes 3551236
  599.6 338.5 %copy-start = (bf16[1088,1024]{1,0:T(8,128)(2,1)S(1)}, bf16[1088,1024]{1,0:T(8,128)(2,1)}, u32[]{:S(2)}) copy-start(bf16[1088,1024]{1,0:T(8,128)(2,1)} %param.1) | copy-start | bytes 6684676
Sparse Core Ops, SparseCore 0:
  8.9 345.4 all-gather.6
  363.8 161.2 all-reduce.1
  543.2 39.2 all-gather.14
  584.6 145.2 all-gather.8
  731.3 59.4 all-gather.12
  792.8 145.2 all-gather.10
where the time goes:
time: 962 us
  waiting for transfers between devices  875 us (91%)
  matrix products  46.4 us (5%)
  local copies, waits for them, and re-layouts  17 us (2%)
  between operations  13.5 us (1%)
    all_gather x1, waiting for transfers between devices, shards(): row_panel = lax.all_gather(gradient, 'col', axis=1, tiled=True)  347 us
    psum x1, waiting for transfers between devices, spread(): return lax.psum(kept, axis)  161 us
    all_gather x1, waiting for transfers between devices, shards(): lax.all_gather(poly_tile, 'col', axis=1, tiled=True)  147 us
    all_gather x1, waiting for transfers between devices, shards(): gram_panel = lax.all_gather(gram_tile, 'col', axis=1, tiled=True)  130 us
    all_gather x1, waiting for transfers between devices, shards(): column_panel = lax.all_gather(gradient, 'row', axis=0, tiled=True)  49 us
    all_gather x1, waiting for transfers between devices, shards(): gram_columns = lax.all_gather(gram_tile, 'row', axis=0, tiled=True)  38.1 us
  transfers between devices with their start and end apart: 6, of which 6 were waited for; matrix products, arithmetic and copies ran while one was open for 3% of the time, Pallas kernels for 0%

commit v1 on v0

v1 whole, which is shorter than its diff:
```python
import math

import jax
import jax.numpy as jnp
from jax import lax
from jax.sharding import PartitionSpec as P

A_COEF = 3.4445
B_COEF = -4.775
C_COEF = 2.0315

ROWS_BY_ROWS = (((1,), (1,)), ((), ()))
PLAIN = (((1,), (0,)), ((), ()))
LEFT_TURNED = (((0,), (0,)), ((), ()))


def product(left, right, dims):
    return lax.dot_general(left, right, dims, preferred_element_type=jnp.float32)


def from_row(value, source):
    count = lax.axis_size("row")
    return lax.ppermute(value, "row", [(source(i), i) for i in range(count)])


def from_col(value, mask):
    count = lax.axis_size("col")
    return lax.ppermute(value, "col", [(i ^ mask, i) for i in range(count)])


def partner(mate):
    top = 1 << (mate.bit_length() - 1)
    return lambda i: i ^ mate ^ (1 if i & top else 0)


def shards(gradient):
    rows = gradient.shape[0]
    row_count = lax.axis_size("row")
    col_count = lax.axis_size("col")
    z_count = col_count // 2
    half = rows // 2
    quarter = half // z_count
    col = lax.axis_index("col")
    y, z = col % 2, col // 2
    mates = range(2, row_count, 2)

    crossed = [from_row(gradient, partner(m)) for m in mates]
    mine = lax.dynamic_slice_in_dim(gradient, y * half, half, 0)
    other = lax.dynamic_slice_in_dim(gradient, (1 - y) * half, half, 0)

    def scatter(right):
        sent = product(other, right, ROWS_BY_ROWS).astype(jnp.bfloat16)
        got = from_col(sent, 1)
        pair = (product(mine, right, ROWS_BY_ROWS) + got.astype(jnp.float32)).astype(jnp.bfloat16)
        total = lax.dynamic_slice_in_dim(pair, z * quarter, quarter, 0).astype(jnp.float32)
        for m in range(1, z_count):
            piece = lax.dynamic_slice_in_dim(pair, (z ^ m) * quarter, quarter, 0)
            total = total + from_col(piece, 2 * m).astype(jnp.float32)
        return total.astype(jnp.bfloat16)

    def gather(shard):
        held = jnp.zeros((half, shard.shape[1]), shard.dtype)
        held = lax.dynamic_update_slice_in_dim(held, shard, z * quarter, 0)
        for m in range(1, z_count):
            held = lax.dynamic_update_slice_in_dim(held, from_col(shard, 2 * m), (z ^ m) * quarter, 0)
        return held, from_col(held, 1)

    def whole(mine_half, other_half):
        first = jnp.where(y == 0, mine_half, other_half)
        second = jnp.where(y == 0, other_half, mine_half)
        return jnp.concatenate([first, second], 0)

    swap = lambda value: from_row(value, lambda i: i ^ 1)
    beside = swap(gradient)
    near = [gradient, beside]
    near_shards = [scatter(right) for right in near]
    near_blocks = [gather(shard) for shard in near_shards]
    far_shards = [scatter(right) for right in crossed]
    turned_shards = [from_row(shard, lambda i, m=m: _inverse(partner(m), row_count)[i]) for m, shard in zip(mates, far_shards)]
    turned = [whole(*gather(shard)) for shard in turned_shards]
    far_blocks = [gather(shard) for shard in far_shards]
    crossed_beside = [swap(value) for value in crossed]

    def rows_times(at, values, turned_sum):
        own, next_to, over, over_beside = values
        total = turned_sum
        for block, right in zip(near_blocks + far_blocks, [own, next_to] + over):
            total = total + product(block[at], right, PLAIN)
        return total

    turned_sum = sum(product(block, right, LEFT_TURNED) for block, right in zip(turned, crossed_beside))
    values = (gradient, beside, crossed, crossed_beside)

    def of_half(value, at):
        return lax.dynamic_slice_in_dim(value, (y if at == 0 else 1 - y) * half, half, 0)

    inner = []
    for at in (0, 1):
        start = of_half(gradient, at).astype(jnp.float32)
        inner.append((B_COEF * start + C_COEF * rows_times(at, values, of_half(turned_sum, at))).astype(jnp.bfloat16))
    inner_crossed = [whole(*[from_row(part, partner(m)) for part in inner]) for m in mates]
    inner_own = whole(*inner)
    inner_values = (inner_own, swap(inner_own), inner_crossed, [swap(value) for value in inner_crossed])
    turned_sum = sum(product(block, right, LEFT_TURNED) for block, right in zip(turned, inner_values[3]))
    rms_scale = math.sqrt(gradient.shape[1] * col_count)
    out = []
    for at in (0, 1):
        start = of_half(gradient, at).astype(jnp.float32)
        out.append((rms_scale * (A_COEF * start + rows_times(at, inner_values, of_half(turned_sum, at)))).astype(jnp.bfloat16))
    return whole(*out)


def _inverse(source, count):
    table = {source(i): i for i in range(count)}
    return [table[i] for i in range(count)]


def solution(mesh):
    spec = P("row", "col")
    return jax.shard_map(shards, mesh=mesh, in_specs=(spec,), out_specs=spec, check_vma=False)
```

time: 962 us -> 400 us (0.42)
  the two profiles are of different devices: /device:TPU:0 before, /device:TPU:19 now
where the time goes in v1:
time: 400 us; the launch traced here: 399 us
  waiting for transfers between devices  256 us (64%)
  starting transfers between devices  78.9 us (20%)
  matrix products  57.5 us (14%)
  other arithmetic  4.37 us (1%)
    ppermute x28, waiting for transfers between devices, from_col(): return lax.ppermute(value, 'col', [(i ^ mask, i) for i in range(count)])  208 us
    dot_general x20, matrix products, product(): lax.dot_general(left, right, dims, preferred_element_type=jnp.float32)  57.5 us
    ppermute x8, waiting for transfers between devices, from_row(): return lax.ppermute(value, 'row', [(source(i), i) for i in range(count)])  47.8 us
    ppermute x8, starting transfers between devices, from_row(): return lax.ppermute(value, 'row', [(source(i), i) for i in range(count)])  41.2 us
    ppermute x28, starting transfers between devices, from_col(): return lax.ppermute(value, 'col', [(i ^ mask, i) for i in range(count)])  37.7 us
  transfers between devices with their start and end apart: 36, of which 20 were waited for; matrix products, arithmetic and copies ran while one was open for 11% of the time, Pallas kernels for 0%

profile of v1, /device:TPU:19, one launch (start us, length us, event | category | flops | bytes accessed | tf_op | source)
XLA Modules:
  0.0 399.3 jit_solution(5410474300818029351)
XLA Ops:
  0.0 3.8 convolution_convert_fusion.1
  6.6 25.8 %collective-permute-done.11 = bf16[544,1088]{1,0:T(8,128)(2,1)} collective-permute-done((bf16[544,1088]{1,0:T(8,128)(2,1)S(1)}, bf16[544,1088]{1,0:T(8,128)(2,1)}, u32[]{:S(2)}, u32[]{:S(2)}) %collective-permute-start.11) | collective-permute-done | bytes 1183776 | tf_op jit(solution)/shard_map/ppermute | solution.py:28
  39.9 4.1 %collective-permute-done.12 = bf16[136,1088]{1,0:T(8,128)(2,1)} collective-permute-done((bf16[136,1088]{1,0:T(8,128)(2,1)}, bf16[136,1088]{1,0:T(8,128)(2,1)}, u32[]{:S(2)}, u32[]{:S(2)}) %collective-permute-start.12) | collective-permute-done | bytes 295968 | tf_op jit(solution)/shard_map/ppermute | solution.py:28
  46.1 17.1 %collective-permute-done.13 = bf16[136,1088]{1,0:T(8,128)(2,1)} collective-permute-done((bf16[136,1088]{1,0:T(8,128)(2,1)}, bf16[136,1088]{1,0:T(8,128)(2,1)}, u32[]{:S(2)}, u32[]{:S(2)}) %collective-permute-start.13) | collective-permute-done | bytes 295968 | tf_op jit(solution)/shard_map/ppermute | solution.py:28
  69.2 9.4 %collective-permute-done.15 = bf16[136,1088]{1,0:T(8,128)(2,1)S(1)} collective-permute-done((bf16[136,1088]{1,0:T(8,128)(2,1)S(1)}, bf16[136,1088]{1,0:T(8,128)(2,1)S(1)}, u32[]{:S(2)}, u32[]{:S(2)}) %collective-permute-start.15) | collective-permute-done | bytes 295968 | tf_op jit(solution)/shard_map/ppermute | solution.py:28
  80.0 14.4 %collective-permute-done.17 = bf16[136,1088]{1,0:T(8,128)(2,1)S(1)} collective-permute-done((bf16[136,1088]{1,0:T(8,128)(2,1)S(1)}, bf16[136,1088]{1,0:T(8,128)(2,1)S(1)}, u32[]{:S(2)}, u32[]{:S(2)}) %collective-permute-start.17) | collective-permute-done | bytes 295968 | tf_op jit(solution)/shard_map/ppermute | solution.py:28
  105.5 4.3 %collective-permute-start.10 = (bf16[1088,1024]{1,0:T(8,128)(2,1)}, bf16[1088,1024]{1,0:T(8,128)(2,1)S(1)}, u32[]{:S(2)}, u32[]{:S(2)}) collective-permute-start(bf16[1088,1024]{1,0:T(8,128)(2,1)} %collective-permute-done), channel_id=1, source_target_pairs={{8,0},{0,8},{24,16},{16,24},{9,1},{1,9},{25,17},{17,25},{10,2},{2,... | collective-permute-start | bytes 6684680 | tf_op jit(solution)/shard_map/ppermute | solution.py:23
  109.8 10.4 %collective-permute-done.30 = bf16[544,1088]{1,0:T(8,128)(2,1)} collective-permute-done((bf16[544,1088]{1,0:T(8,128)(2,1)S(1)}, bf16[544,1088]{1,0:T(8,128)(2,1)}, u32[]{:S(2)}, u32[]{:S(2)}) %collective-permute-start.30) | collective-permute-done | bytes 1183776 | tf_op jit(solution)/shard_map/ppermute | solution.py:28
  123.1 23.9 %collective-permute-done.1 = bf16[544,1088]{1,0:T(8,128)(2,1)S(1)} collective-permute-done((bf16[544,1088]{1,0:T(8,128)(2,1)S(1)}, bf16[544,1088]{1,0:T(8,128)(2,1)S(1)}, u32[]{:S(2)}, u32[]{:S(2)}) %collective-permute-start.1) | collective-permute-done | bytes 1183776 | tf_op jit(solution)/shard_map/ppermute | solution.py:28
  154.0 19.9 %collective-permute-done.19 = bf16[544,1088]{1,0:T(8,128)(2,1)S(1)} collective-permute-done((bf16[544,1088]{1,0:T(8,128)(2,1)S(1)}, bf16[544,1088]{1,0:T(8,128)(2,1)S(1)}, u32[]{:S(2)}, u32[]{:S(2)}) %collective-permute-start.19) | collective-permute-done | bytes 1183776 | tf_op jit(solution)/shard_map/ppermute | solution.py:28
  187.0 16.1 %collective-permute-done.21 = bf16[136,1088]{1,0:T(8,128)(2,1)S(1)} collective-permute-done((bf16[136,1088]{1,0:T(8,128)(2,1)S(1)}, bf16[136,1088]{1,0:T(8,128)(2,1)S(1)}, u32[]{:S(2)}, u32[]{:S(2)}) %collective-permute-start.21) | collective-permute-done | bytes 295968 | tf_op jit(solution)/shard_map/ppermute | solution.py:28
  203.1 23.6 %collective-permute-start.5 = (bf16[136,1088]{1,0:T(8,128)(2,1)S(1)}, bf16[136,1088]{1,0:T(8,128)(2,1)S(1)}, u32[]{:S(2)}, u32[]{:S(2)}) collective-permute-start(bf16[136,1088]{1,0:T(8,128)(2,1)S(1)} %get-tuple-element.11), channel_id=1, source_target_pairs={{24,0},{16,8},{0,16},{8,24},{25,1},{17,9},{1,17},{9,25},{26,2},{18... | collective-permute-start | bytes 887816 | tf_op jit(solution)/shard_map/ppermute | solution.py:23
  230.3 7.0 %collective-permute-done.28 = bf16[136,1088]{1,0:T(8,128)(2,1)S(1)} collective-permute-done((bf16[136,1088]{1,0:T(8,128)(2,1)S(1)}, bf16[136,1088]{1,0:T(8,128)(2,1)S(1)}, u32[]{:S(2)}, u32[]{:S(2)}) %collective-permute-start.28) | collective-permute-done | bytes 295968 | tf_op jit(solution)/shard_map/ppermute | solution.py:28
  238.7 5.3 %collective-permute-done.24 = bf16[136,1088]{1,0:T(8,128)(2,1)S(1)} collective-permute-done((bf16[136,1088]{1,0:T(8,128)(2,1)S(1)}, bf16[136,1088]{1,0:T(8,128)(2,1)S(1)}, u32[]{:S(2)}, u32[]{:S(2)}) %collective-permute-start.24) | collective-permute-done | bytes 295968 | tf_op jit(solution)/shard_map/ppermute | solution.py:28
  244.1 13.4 %collective-permute-done.25 = bf16[136,1088]{1,0:T(8,128)(2,1)S(1)} collective-permute-done((bf16[136,1088]{1,0:T(8,128)(2,1)S(1)}, bf16[136,1088]{1,0:T(8,128)(2,1)S(1)}, u32[]{:S(2)}, u32[]{:S(2)}) %collective-permute-start.25) | collective-permute-done | bytes 295968 | tf_op jit(solution)/shard_map/ppermute | solution.py:28
  259.2 7.0 %collective-permute-done.7 = bf16[136,1088]{1,0:T(8,128)(2,1)S(1)} collective-permute-done((bf16[136,1088]{1,0:T(8,128)(2,1)S(1)}, bf16[136,1088]{1,0:T(8,128)(2,1)S(1)}, u32[]{:S(2)}, u32[]{:S(2)}) %collective-permute-start.7) | collective-permute-done | bytes 295968 | tf_op jit(solution)/shard_map/ppermute | solution.py:28
  266.2 9.6 %collective-permute-done.8 = bf16[136,1088]{1,0:T(8,128)(2,1)S(1)} collective-permute-done((bf16[136,1088]{1,0:T(8,128)(2,1)S(1)}, bf16[136,1088]{1,0:T(8,128)(2,1)S(1)}, u32[]{:S(2)}, u32[]{:S(2)}) %collective-permute-start.8) | collective-permute-done | bytes 295968 | tf_op jit(solution)/shard_map/ppermute | solution.py:28
  275.8 9.6 %collective-permute-start.9 = (bf16[544,1088]{1,0:T(8,128)(2,1)S(1)}, bf16[544,1088]{1,0:T(8,128)(2,1)S(1)}, u32[]{:S(2)}, u32[]{:S(2)}) collective-permute-start(bf16[544,1088]{1,0:T(8,128)(2,1)S(1)} %constant_dynamic-update-slice_fusion.12), channel_id=1, source_target_pairs={{1,0},{0,1},{3,2},{2,3},{5,4},{4,5},{7,6},{6,7},{9,8},{8,9},{11,10... | collective-permute-start | bytes 3551240 | tf_op jit(solution)/shard_map/ppermute | solution.py:28
  292.0 3.7 fusion.40
  295.7 18.4 %collective-permute-done.9 = bf16[544,1088]{1,0:T(8,128)(2,1)S(1)} collective-permute-done((bf16[544,1088]{1,0:T(8,128)(2,1)S(1)}, bf16[544,1088]{1,0:T(8,128)(2,1)S(1)}, u32[]{:S(2)}, u32[]{:S(2)}) %collective-permute-start.9) | collective-permute-done | bytes 1183776 | tf_op jit(solution)/shard_map/ppermute | solution.py:28
  317.5 4.5 %broadcast_select_fusion.5 = (bf16[544,1024]{1,0:T(8,128)(2,1)S(1)}, bf16[544,1024]{1,0:T(8,128)(2,1)S(1)}, bf16[544,1024]{1,0:T(8,128)(2,1)S(1)}) fusion(pred[]{:T(512)S(6)} %eq.4, f32[544,1024]{1,0:T(8,128)S(1)} %fusion.38, f32[544,1024]{1,0:T(8,128)S(1)} %fusion.37, f32[1088,1024]{1,0:T(8,128)S(1)} %fusion.13, s32[]{:T(128)S(6)} %select_n.103, ...), kind=kOutput, calls=%fused_computation.33 | convolution fusion | flops 1221623808 | bytes 24580104 | tf_op jit(solution)/shard_map/dot_general | solution.py:18
  323.3 9.4 %collective-permute-start.33 = (bf16[544,1024]{1,0:T(8,128)(2,1)S(1)}, bf16[544,1024]{1,0:T(8,128)(2,1)S(1)}, u32[]{:S(2)}, u32[]{:S(2)}) collective-permute-start(bf16[544,1024]{1,0:T(8,128)(2,1)S(1)} %get-tuple-element.7), channel_id=1, source_target_pairs={{16,0},{24,8},{8,16},{0,24},{17,1},{25,9},{9,17},{1,25},{18,2},{26... | collective-permute-start | bytes 3342344 | tf_op jit(solution)/shard_map/ppermute | solution.py:23
  333.6 24.4 %collective-permute-done.29 = bf16[544,1024]{1,0:T(8,128)(2,1)S(1)} collective-permute-done((bf16[544,1024]{1,0:T(8,128)(2,1)S(1)}, bf16[544,1024]{1,0:T(8,128)(2,1)S(1)}, u32[]{:S(2)}, u32[]{:S(2)}) %collective-permute-start.29) | collective-permute-done | bytes 1114144 | tf_op jit(solution)/shard_map/ppermute | solution.py:23
  358.0 23.4 %collective-permute-done.33 = bf16[544,1024]{1,0:T(8,128)(2,1)S(1)} collective-permute-done((bf16[544,1024]{1,0:T(8,128)(2,1)S(1)}, bf16[544,1024]{1,0:T(8,128)(2,1)S(1)}, u32[]{:S(2)}, u32[]{:S(2)}) %collective-permute-start.33) | collective-permute-done | bytes 1114144 | tf_op jit(solution)/shard_map/ppermute | solution.py:23
  (105 shorter events, 90.5 us)
Async XLA Ops:
  3.8 28.6 %collective-permute-start.11 = (bf16[544,1088]{1,0:T(8,128)(2,1)S(1)}, bf16[544,1088]{1,0:T(8,128)(2,1)}, u32[]{:S(2)}, u32[]{:S(2)}) collective-permute-start(bf16[544,1088]{1,0:T(8,128)(2,1)S(1)} %convolution_convert_fusion.1), channel_id=1, source_target_pairs={{1,0},{0,1},{3,2},{2,3},{5,4},{4,5},{7,6},{6,7},{9,8},{8,9},{11,10... | collective-permute-start | bytes 3551240 | tf_op jit(solution)/shard_map/ppermute | solution.py:28
  5.1 90.6 %collective-permute-start = (bf16[1088,1024]{1,0:T(8,128)(2,1)S(1)}, bf16[1088,1024]{1,0:T(8,128)(2,1)}, u32[]{:S(2)}, u32[]{:S(2)}) collective-permute-start(bf16[1088,1024]{1,0:T(8,128)(2,1)S(1)} %copy-done), channel_id=1, source_target_pairs={{16,0},{24,8},{8,16},{0,24},{17,1},{25,9},{9,17},{1,25},{18,2},{26... | collective-permute-start | bytes 6684680 | tf_op jit(solution)/shard_map/ppermute | solution.py:23
  5.3 94.0 %collective-permute-start.18 = (bf16[1088,1024]{1,0:T(8,128)(2,1)S(1)}, bf16[1088,1024]{1,0:T(8,128)(2,1)}, u32[]{:S(2)}, u32[]{:S(2)}) collective-permute-start(bf16[1088,1024]{1,0:T(8,128)(2,1)S(1)} %copy-done), channel_id=1, source_target_pairs={{8,0},{0,8},{24,16},{16,24},{9,1},{1,9},{25,17},{17,25},{10,2},{2,... | collective-permute-start | bytes 6684680 | tf_op jit(solution)/shard_map/ppermute | solution.py:23
  37.7 25.6 %collective-permute-start.13 = (bf16[136,1088]{1,0:T(8,128)(2,1)}, bf16[136,1088]{1,0:T(8,128)(2,1)}, u32[]{:S(2)}, u32[]{:S(2)}) collective-permute-start(bf16[136,1088]{1,0:T(8,128)(2,1)} %get-tuple-element.22), channel_id=1, source_target_pairs={{4,0},{5,1},{6,2},{7,3},{0,4},{1,5},{2,6},{3,7},{12,8},{13,9},{14,... | collective-permute-start | bytes 887816 | tf_op jit(solution)/shard_map/ppermute | solution.py:28
  68.0 26.3 %collective-permute-start.17 = (bf16[136,1088]{1,0:T(8,128)(2,1)S(1)}, bf16[136,1088]{1,0:T(8,128)(2,1)S(1)}, u32[]{:S(2)}, u32[]{:S(2)}) collective-permute-start(bf16[136,1088]{1,0:T(8,128)(2,1)S(1)} %get-tuple-element.9), channel_id=1, source_target_pairs={{6,0},{7,1},{4,2},{5,3},{2,4},{3,5},{0,6},{1,7},{14,8},{15,9},{12,... | collective-permute-start | bytes 887816 | tf_op jit(solution)/shard_map/ppermute | solution.py:28
  94.4 25.8 %collective-permute-start.30 = (bf16[544,1088]{1,0:T(8,128)(2,1)S(1)}, bf16[544,1088]{1,0:T(8,128)(2,1)}, u32[]{:S(2)}, u32[]{:S(2)}) collective-permute-start(bf16[544,1088]{1,0:T(8,128)(2,1)S(1)} %constant_dynamic-update-slice_fusion.8), channel_id=1, source_target_pairs={{1,0},{0,1},{3,2},{2,3},{5,4},{4,5},{7,6},{6,7},{9,8},{8,9},{11,10... | collective-permute-start | bytes 3551240 | tf_op jit(solution)/shard_map/ppermute | solution.py:28
  99.0 48.0 %collective-permute-start.1 = (bf16[544,1088]{1,0:T(8,128)(2,1)S(1)}, bf16[544,1088]{1,0:T(8,128)(2,1)S(1)}, u32[]{:S(2)}, u32[]{:S(2)}) collective-permute-start(bf16[544,1088]{1,0:T(8,128)(2,1)S(1)} %convolution_convert_fusion.2), channel_id=1, source_target_pairs={{1,0},{0,1},{3,2},{2,3},{5,4},{4,5},{7,6},{6,7},{9,8},{8,9},{11,10... | collective-permute-start | bytes 3551240 | tf_op jit(solution)/shard_map/ppermute | solution.py:28
  102.6 71.3 %collective-permute-start.19 = (bf16[544,1088]{1,0:T(8,128)(2,1)S(1)}, bf16[544,1088]{1,0:T(8,128)(2,1)S(1)}, u32[]{:S(2)}, u32[]{:S(2)}) collective-permute-start(bf16[544,1088]{1,0:T(8,128)(2,1)S(1)} %convolution_convert_fusion), channel_id=1, source_target_pairs={{1,0},{0,1},{3,2},{2,3},{5,4},{4,5},{7,6},{6,7},{9,8},{8,9},{11,10... | collective-permute-start | bytes 3551240 | tf_op jit(solution)/shard_map/ppermute | solution.py:28
  105.5 208.8 %collective-permute-start.10 = (bf16[1088,1024]{1,0:T(8,128)(2,1)}, bf16[1088,1024]{1,0:T(8,128)(2,1)S(1)}, u32[]{:S(2)}, u32[]{:S(2)}) collective-permute-start(bf16[1088,1024]{1,0:T(8,128)(2,1)} %collective-permute-done), channel_id=1, source_target_pairs={{8,0},{0,8},{24,16},{16,24},{9,1},{1,9},{25,17},{17,25},{10,2},{2,... | collective-permute-start | bytes 6684680 | tf_op jit(solution)/shard_map/ppermute | solution.py:23
  150.4 26.9 %collective-permute-start.2 = (bf16[136,1088]{1,0:T(8,128)(2,1)S(1)}, bf16[136,1088]{1,0:T(8,128)(2,1)S(1)}, u32[]{:S(2)}, u32[]{:S(2)}) collective-permute-start(bf16[136,1088]{1,0:T(8,128)(2,1)S(1)} %get-tuple-element.23), channel_id=1, source_target_pairs={{2,0},{3,1},{0,2},{1,3},{6,4},{7,5},{4,6},{5,7},{10,8},{11,9},{8,1... | collective-permute-start | bytes 887816 | tf_op jit(solution)/shard_map/ppermute | solution.py:28
  150.4 26.9 %collective-permute-start.4 = (bf16[136,1088]{1,0:T(8,128)(2,1)S(1)}, bf16[136,1088]{1,0:T(8,128)(2,1)S(1)}, u32[]{:S(2)}, u32[]{:S(2)}) collective-permute-start(bf16[136,1088]{1,0:T(8,128)(2,1)S(1)} %get-tuple-element.24), channel_id=1, source_target_pairs={{6,0},{7,1},{4,2},{5,3},{2,4},{3,5},{0,6},{1,7},{14,8},{15,9},{12,... | collective-permute-start | bytes 887816 | tf_op jit(solution)/shard_map/ppermute | solution.py:28
  150.5 30.3 %collective-permute-start.3 = (bf16[136,1088]{1,0:T(8,128)(2,1)S(1)}, bf16[136,1088]{1,0:T(8,128)(2,1)S(1)}, u32[]{:S(2)}, u32[]{:S(2)}) collective-permute-start(bf16[136,1088]{1,0:T(8,128)(2,1)S(1)} %get-tuple-element.25), channel_id=1, source_target_pairs={{4,0},{5,1},{6,2},{7,3},{0,4},{1,5},{2,6},{3,7},{12,8},{13,9},{14,... | collective-permute-start | bytes 887816 | tf_op jit(solution)/shard_map/ppermute | solution.py:28
  177.4 25.7 %collective-permute-start.21 = (bf16[136,1088]{1,0:T(8,128)(2,1)S(1)}, bf16[136,1088]{1,0:T(8,128)(2,1)S(1)}, u32[]{:S(2)}, u32[]{:S(2)}) collective-permute-start(bf16[136,1088]{1,0:T(8,128)(2,1)S(1)} %get-tuple-element.28), channel_id=1, source_target_pairs={{4,0},{5,1},{6,2},{7,3},{0,4},{1,5},{2,6},{3,7},{12,8},{13,9},{14,... | collective-permute-start | bytes 887816 | tf_op jit(solution)/shard_map/ppermute | solution.py:28
  181.1 49.1 %collective-permute-start.27 = (bf16[136,1088]{1,0:T(8,128)(2,1)S(1)}, bf16[136,1088]{1,0:T(8,128)(2,1)S(1)}, u32[]{:S(2)}, u32[]{:S(2)}) collective-permute-start(bf16[136,1088]{1,0:T(8,128)(2,1)S(1)} %get-tuple-element.11), channel_id=1, source_target_pairs={{4,0},{5,1},{6,2},{7,3},{0,4},{1,5},{2,6},{3,7},{12,8},{13,9},{14,... | collective-permute-start | bytes 887816 | tf_op jit(solution)/shard_map/ppermute | solution.py:28
  184.3 42.7 %collective-permute-start.26 = (bf16[136,1088]{1,0:T(8,128)(2,1)S(1)}, bf16[136,1088]{1,0:T(8,128)(2,1)S(1)}, u32[]{:S(2)}, u32[]{:S(2)}) collective-permute-start(bf16[136,1088]{1,0:T(8,128)(2,1)S(1)} %get-tuple-element.11), channel_id=1, source_target_pairs={{2,0},{3,1},{0,2},{1,3},{6,4},{7,5},{4,6},{5,7},{10,8},{11,9},{8,1... | collective-permute-start | bytes 887816 | tf_op jit(solution)/shard_map/ppermute | solution.py:28
  186.9 50.4 %collective-permute-start.28 = (bf16[136,1088]{1,0:T(8,128)(2,1)S(1)}, bf16[136,1088]{1,0:T(8,128)(2,1)S(1)}, u32[]{:S(2)}, u32[]{:S(2)}) collective-permute-start(bf16[136,1088]{1,0:T(8,128)(2,1)S(1)} %get-tuple-element.11), channel_id=1, source_target_pairs={{6,0},{7,1},{4,2},{5,3},{2,4},{3,5},{0,6},{1,7},{14,8},{15,9},{12,... | collective-permute-start | bytes 887816 | tf_op jit(solution)/shard_map/ppermute | solution.py:28
  203.1 34.3 %collective-permute-start.5 = (bf16[136,1088]{1,0:T(8,128)(2,1)S(1)}, bf16[136,1088]{1,0:T(8,128)(2,1)S(1)}, u32[]{:S(2)}, u32[]{:S(2)}) collective-permute-start(bf16[136,1088]{1,0:T(8,128)(2,1)S(1)} %get-tuple-element.11), channel_id=1, source_target_pairs={{24,0},{16,8},{0,16},{8,24},{25,1},{17,9},{1,17},{9,25},{26,2},{18... | collective-permute-start | bytes 887816 | tf_op jit(solution)/shard_map/ppermute | solution.py:23
  237.4 51.3 %collective-permute-start.32 = (bf16[544,1088]{1,0:T(8,128)(2,1)S(1)}, bf16[544,1088]{1,0:T(8,128)(2,1)S(1)}, u32[]{:S(2)}, u32[]{:S(2)}) collective-permute-start(bf16[544,1088]{1,0:T(8,128)(2,1)S(1)} %constant_dynamic-update-slice_fusion), channel_id=1, source_target_pairs={{1,0},{0,1},{3,2},{2,3},{5,4},{4,5},{7,6},{6,7},{9,8},{8,9},{11,10... | collective-permute-start | bytes 3551240 | tf_op jit(solution)/shard_map/ppermute | solution.py:28
  238.7 20.3 %collective-permute-start.6 = (bf16[136,1088]{1,0:T(8,128)(2,1)S(1)}, bf16[136,1088]{1,0:T(8,128)(2,1)S(1)}, u32[]{:S(2)}, u32[]{:S(2)}) collective-permute-start(bf16[136,1088]{1,0:T(8,128)(2,1)S(1)} %collective-permute-done.5), channel_id=1, source_target_pairs={{2,0},{3,1},{0,2},{1,3},{6,4},{7,5},{4,6},{5,7},{10,8},{11,9},{8,1... | collective-permute-start | bytes 887816 | tf_op jit(solution)/shard_map/ppermute | solution.py:28
  257.5 34.4 %collective-permute-start.31 = (bf16[544,1088]{1,0:T(8,128)(2,1)S(1)}, bf16[544,1088]{1,0:T(8,128)(2,1)S(1)}, u32[]{:S(2)}, u32[]{:S(2)}) collective-permute-start(bf16[544,1088]{1,0:T(8,128)(2,1)S(1)} %constant_dynamic-update-slice_fusion.4), channel_id=1, source_target_pairs={{1,0},{0,1},{3,2},{2,3},{5,4},{4,5},{7,6},{6,7},{9,8},{8,9},{11,10... | collective-permute-start | bytes 3551240 | tf_op jit(solution)/shard_map/ppermute | solution.py:28
  275.8 38.2 %collective-permute-start.9 = (bf16[544,1088]{1,0:T(8,128)(2,1)S(1)}, bf16[544,1088]{1,0:T(8,128)(2,1)S(1)}, u32[]{:S(2)}, u32[]{:S(2)}) collective-permute-start(bf16[544,1088]{1,0:T(8,128)(2,1)S(1)} %constant_dynamic-update-slice_fusion.12), channel_id=1, source_target_pairs={{1,0},{0,1},{3,2},{2,3},{5,4},{4,5},{7,6},{6,7},{9,8},{8,9},{11,10... | collective-permute-start | bytes 3551240 | tf_op jit(solution)/shard_map/ppermute | solution.py:28
  322.0 36.0 %collective-permute-start.29 = (bf16[544,1024]{1,0:T(8,128)(2,1)S(1)}, bf16[544,1024]{1,0:T(8,128)(2,1)S(1)}, u32[]{:S(2)}, u32[]{:S(2)}) collective-permute-start(bf16[544,1024]{1,0:T(8,128)(2,1)S(1)} %get-tuple-element.6), channel_id=1, source_target_pairs={{16,0},{24,8},{8,16},{0,24},{17,1},{25,9},{9,17},{1,25},{18,2},{26... | collective-permute-start | bytes 3342344 | tf_op jit(solution)/shard_map/ppermute | solution.py:23
  323.3 58.1 %collective-permute-start.33 = (bf16[544,1024]{1,0:T(8,128)(2,1)S(1)}, bf16[544,1024]{1,0:T(8,128)(2,1)S(1)}, u32[]{:S(2)}, u32[]{:S(2)}) collective-permute-start(bf16[544,1024]{1,0:T(8,128)(2,1)S(1)} %get-tuple-element.7), channel_id=1, source_target_pairs={{16,0},{24,8},{8,16},{0,24},{17,1},{25,9},{9,17},{1,25},{18,2},{26... | collective-permute-start | bytes 3342344 | tf_op jit(solution)/shard_map/ppermute | solution.py:23
  333.0 54.0 %collective-permute-start.35 = (bf16[1088,1024]{1,0:T(8,128)(2,1)S(1)}, bf16[1088,1024]{1,0:T(8,128)(2,1)S(1)}, u32[]{:S(2)}, u32[]{:S(2)}) collective-permute-start(bf16[1088,1024]{1,0:T(8,128)(2,1)S(1)} %pad_maximum_fusion.2), channel_id=1, source_target_pairs={{8,0},{0,8},{24,16},{16,24},{9,1},{1,9},{25,17},{17,25},{10,2},{2,... | collective-permute-start | bytes 6684680 | tf_op jit(solution)/shard_map/ppermute | solution.py:23
  (16 other events, 159.5 us)

commit v2 on v0

v2 whole, which is shorter than its diff:
```python
import heapq
import math

import jax
import jax.numpy as jnp
from jax import lax
from jax.sharding import PartitionSpec as P

A_COEF = 3.4445
B_COEF = -4.775
C_COEF = 2.0315

ROWS_BY_ROWS = (((1,), (1,)), ((), ()))
PLAIN = (((1,), (0,)), ((), ()))
LEFT_TURNED = (((0,), (0,)), ((), ()))

STEP_COST = 7.0
NEAR_COST = 60.0
FAR_COST = 50.0
BESIDE_COST = 9.0
CROSSED_COST = 50.0
CROSSED_BESIDE_AT = 90.0


def product(left, right, dims):
    return lax.dot_general(left, right, dims, preferred_element_type=jnp.float32)


def from_row(value, source):
    count = lax.axis_size("row")
    return lax.ppermute(value, "row", [(source(i), i) for i in range(count)])


def from_col(value, mask):
    count = lax.axis_size("col")
    return lax.ppermute(value, "col", [(i ^ mask, i) for i in range(count)])


def swap(value):
    return from_row(value, lambda i: i ^ 1)


def partner(mate):
    top = 1 << (mate.bit_length() - 1)
    return lambda i: i ^ mate ^ (1 if i & top else 0)


def inverse(source, count):
    table = {source(i): i for i in range(count)}
    return table.__getitem__


class Sequence:
    def __init__(self):
        self.last = None
        self.agenda = []
        self.added = 0

    def __call__(self, name, step, *values):
        if self.last is not None:
            values = lax.optimization_barrier((values, self.last))[0]
        with jax.named_scope(name):
            result = step(*values)
        self.last = jax.tree.leaves(result)[0]
        return result

    def hold(self, value):
        value, _ = lax.optimization_barrier((value, self.last))
        self.last = value
        return value

    def at(self, time, step):
        heapq.heappush(self.agenda, (time, self.added, step))
        self.added += 1

    def drain(self):
        while self.agenda:
            time, _, step = heapq.heappop(self.agenda)
            step(time)


def take(value, at, count):
    return lax.dynamic_slice_in_dim(value, at * count, count, 0)


def joined(mine, other, at, axis=0):
    count = mine.shape[axis]
    shape = mine.shape[:axis] + (2 * count,) + mine.shape[axis + 1 :]
    both = lax.dynamic_update_slice_in_dim(jnp.zeros(shape, mine.dtype), mine, at * count, axis)
    if other is None:
        return both
    return lax.dynamic_update_slice_in_dim(both, other, (1 - at) * count, axis)


class Scatter:
    def __init__(self, run, name, masks, cost, left, right, bit, done):
        self.cost, self.run, self.name, self.masks, self.left, self.right, self.bit, self.done = cost, run, name, masks, left, right, bit, done
        self.share = right.shape[0] / left.shape[0]

    def start(self, time):
        mask, half = self.masks[0], self.left.shape[0] // 2
        at = self.bit(mask)

        def sent(left, right):
            return product(take(left, 1 - at, half), right, ROWS_BY_ROWS).astype(jnp.bfloat16)

        def kept(left, right):
            return product(take(left, at, half), right, ROWS_BY_ROWS)

        self.got = from_col(self.run(self.name + "_sent", sent, self.left, self.right), mask)
        self.kept = self.run(self.name + "_kept", kept, self.left, self.right)
        self.step = 1
        self.run.at(time + STEP_COST + self.cost * self.share / 2, self.halve)

    def halve(self, time):
        if self.step == len(self.masks):
            shard = self.run(self.name + "_shard", lambda kept, got: (kept + got.astype(jnp.float32)).astype(jnp.bfloat16), self.kept, self.got)
            return self.done(time, shard)
        mask, count = self.masks[self.step], self.kept.shape[0] // 2
        at = self.bit(mask)

        def one(kept, got):
            total = kept + got.astype(jnp.float32)
            return take(total, 1 - at, count).astype(jnp.bfloat16), take(total, at, count)

        sent, self.kept = self.run(f"{self.name}_halved_{self.step}", one, self.kept, self.got)
        self.got = from_col(sent, mask)
        self.step += 1
        self.run.at(time + STEP_COST + self.cost * self.share / 2**self.step, self.halve)


class Gather:
    def __init__(self, run, name, masks, steps, cost, bit, shard, done=None, stop=0):
        self.run, self.name, self.masks, self.steps, self.bit, self.done, self.stop = run, name, masks, list(steps), bit, done, stop
        self.held = shard.reshape((1,) * len(masks) + shard.shape)
        self.share = cost * shard.shape[1] / shard.shape[0] / 4 ** len(masks)

    def start(self, time):
        if self.done is not None and len(self.steps) == self.stop:
            self.done(time)
        if self.steps:
            self.got = from_col(self.held, self.steps[0])
            if len(self.steps) > self.stop:
                self.run.at(time + STEP_COST + self.share, self.double)

    def double(self, time):
        mask = self.steps.pop(0)
        axis, at = self.masks.index(mask), self.bit(mask)
        self.held = self.run(f"{self.name}_doubled_{len(self.steps)}", lambda held, got: joined(held, got, at, axis), self.held, self.got)
        self.share *= 2
        self.start(time)

    @property
    def block(self):
        return self.held.reshape(-1, self.held.shape[-1])


def shards(gradient):
    kept_rows = gradient.shape[0]
    row_count = lax.axis_size("row")
    col_count = lax.axis_size("col")
    gradient = jnp.pad(gradient, ((0, -kept_rows % col_count), (0, 0)))
    rows = gradient.shape[0]
    half = rows // 2
    col = lax.axis_index("col")
    masks = [1 << b for b in range(col_count.bit_length() - 1)]
    y_first, z_first = masks, masks[1:] + masks[:1]
    y_last = masks[::-1]
    z_last = masks[:1] + masks[:0:-1]
    mates = range(2, row_count, 2)
    run = Sequence()

    def bit(mask):
        return col // mask % 2

    at = bit(masks[0])
    cut = half // 128 * 128
    bounds = [(0, cut), (cut, rows)] if cut else [(0, rows)]
    beside = swap(gradient)
    sent_parts = []

    def send_part(time):
        a, b = bounds[len(sent_parts)]
        sent_parts.append(run("part", lambda value: value[a:b], gradient))

    send_part(0)
    own = Scatter(run, "own", z_first, NEAR_COST, gradient, gradient, bit, lambda time, shard: gather("own", z_first, y_last, NEAR_COST, done=add_inner("own", "own", gradient))(time, shard))
    own.start(0)
    for _ in bounds[1:]:
        send_part(0)
    crossed_parts = [[from_row(part, partner(m)) for part in sent_parts] for m in mates]
    crossed_beside_parts = [[None] * len(bounds) for m in mates]
    gathers = {}
    turned = {}
    inner = []

    def add_inner(name, left, right):
        def add(time):
            block = gathers[name].block
            if inner:
                inner[0] = run("inner_" + name, lambda total, block, right: total + product(block, right, PLAIN), inner[0], block, right)
            else:
                inner.append(run("inner_" + name, lambda block, right: product(block, right, PLAIN), block, right))

        return add

    def gather(name, masks, steps, cost, stop=0, done=None):
        def begin(time, shard):
            gathers[name] = Gather(run, name, masks, steps, cost, bit, shard, stop=stop, done=done)
            gathers[name].start(time)

        return begin

    def part_done(m, index):
        name = f"far_{m}_{index}"
        source = inverse(partner(m), row_count)

        def over(value, time, place):
            moved = from_row(value, source)
            run.at(time + STEP_COST + CROSSED_COST / 4, lambda time: turned.__setitem__((m, index, place), run.hold(moved)))

        def arrived(time):
            piece = gathers[name]
            piece.got = run.hold(piece.got)
            over(piece.got, time, 1)

        def mine_done(time):
            over(gathers[name].held, time, 0)
            run.at(time + STEP_COST + FAR_COST / 4, arrived)

        return lambda time, shard: gather(name, y_first, y_last, FAR_COST, stop=1, done=mine_done)(time, shard)

    def far_start(m, index, part):
        scatter = Scatter(run, f"far_{m}_{index}", y_first, FAR_COST, gradient, part, bit, part_done(m, index))

        def start(time):
            scatter.start(time)

        return start

    def start_beside(time):
        for values, kept in zip(crossed_parts, crossed_beside_parts):
            for index, value in enumerate(values):
                run.at(time + 2 * BESIDE_COST, lambda time, kept=kept, index=index, value=swap(run.hold(value)): kept.__setitem__(index, run.hold(value)))

    run.at(CROSSED_BESIDE_AT, start_beside)
    run.at(BESIDE_COST, Scatter(run, "next", y_first, NEAR_COST, gradient, beside, bit, gather("next", y_first, z_last, NEAR_COST, done=add_inner("next", "next", beside))).start)
    for m, parts in zip(mates, crossed_parts):
        for index, (part, (_, end)) in enumerate(zip(parts, bounds)):
            run.at(STEP_COST + CROSSED_COST * end / rows, far_start(m, index, part))
    run.drain()

    inner = inner[0]
    own, near = gathers["own"].block, gathers["next"].block
    parts = range(len(bounds))
    beside_columns = lambda *values: jnp.concatenate(values, -1)
    whole_columns = lambda *values: joined(*[jnp.concatenate(values[i :: 2], -1).reshape(half, rows) for i in (0, 1)], at)
    turned = [run("turned_whole", whole_columns, *[turned[m, i, place] for i in parts for place in (0, 1)]) for m in mates]
    below = lambda *values: jnp.concatenate(values, 0)
    crossed_beside = [run("crossed_beside_whole", below, *values) for values in crossed_beside_parts]
    for block, right in zip(turned, crossed_beside):
        inner = run("inner_turned", lambda total, block, right: total + product(block, right, LEFT_TURNED), inner, block, right)
    crossed = [run("crossed_whole", below, *values) for values in crossed_parts]
    far_mine = [run("far_mine", beside_columns, *[gathers[f"far_{m}_{i}"].held.reshape(half, -1) for i in parts]) for m in mates]

    def finish_inner(total, start, side, *blocks):
        total = take(total, side, half)
        for block, right in zip(blocks, crossed):
            total = total + product(block, right, PLAIN)
        return (B_COEF * take(start, side, half).astype(jnp.float32) + C_COEF * total).astype(jnp.bfloat16)

    mine = run("inner_mine", lambda total, start, *blocks: finish_inner(total, start, at, *blocks), inner, gradient, *far_mine)
    mine_crossed = [from_row(mine, partner(m)) for m in mates]
    far_other = [run("far_other", beside_columns, *[gathers[f"far_{m}_{i}"].got.reshape(half, -1) for i in parts]) for m in mates]
    other = run("inner_other", lambda total, start, *blocks: finish_inner(total, start, 1 - at, *blocks), inner, gradient, *far_other)
    other_crossed = [from_row(other, partner(m)) for m in mates]
    inner = run("inner_whole", lambda a, b: joined(a, b, at), mine, other)
    inner_beside = swap(inner)
    far = [run("far_whole", lambda a, b: joined(a, b, at), a, b) for a, b in zip(far_mine, far_other)]
    mine_crossed = [run.hold(value) for value in mine_crossed]
    mine_beside = [swap(value) for value in mine_crossed]
    outer = run("outer_own", lambda block, right: product(block, right, PLAIN), own, inner)
    outer = run("outer_next", lambda total, block, right: total + product(block, right, PLAIN), outer, near, inner_beside)

    def add_far(total, block, right, side):
        return total + product(block, joined(right, None, side), PLAIN)

    for block, right in zip(far, mine_crossed):
        outer = run("outer_far_mine", lambda total, block, right: add_far(total, block, right, at), outer, block, right)
    for block, right in zip(turned, mine_beside):
        outer = run("outer_turned_mine", lambda total, block, right: total + product(take(block, at, half), right, LEFT_TURNED), outer, block, right)
    other_crossed = [run.hold(value) for value in other_crossed]
    other_beside = [swap(value) for value in other_crossed]
    for block, right in zip(far, other_crossed):
        outer = run("outer_far_other", lambda total, block, right: add_far(total, block, right, 1 - at), outer, block, right)
    rms_scale = math.sqrt(gradient.shape[1] * col_count)

    def finish_outer(total, start, *pairs):
        count = len(pairs) // 2
        for block, right in zip(pairs[:count], pairs[count:]):
            total = total + product(take(block, 1 - at, half), right, LEFT_TURNED)
        return (rms_scale * (A_COEF * start.astype(jnp.float32) + total)).astype(jnp.bfloat16)

    return run("update", finish_outer, outer, gradient, *turned, *other_beside)[:kept_rows]


def solution(mesh):
    spec = P("row", "col")
    return jax.shard_map(shards, mesh=mesh, in_specs=(spec,), out_specs=spec, check_vma=False)
```

time: 962 us -> 317 us (0.33)
  waiting for transfers between devices: 875 us -> 164 us
  starting transfers between devices: 0.38 us -> 69.5 us
  between operations: 13.5 us -> 1.25 us
    all_gather x5 -> x0, waiting for transfers between devices: 712 us -> none  [the longest x1 347 us: shards(): row_panel = lax.all_gather(gradient, 'col', axis=1, tiled=True)]
    ppermute x0 -> x38, waiting for transfers between devices: none -> 164 us  [the longest x24 95 us: from_col(): return lax.ppermute(value, 'col', [(i ^ mask, i) for i in range(count)])]
    psum x1 -> x0, waiting for transfers between devices: 161 us -> none  [spread(): return lax.psum(kept, axis)]
    ppermute x0 -> x38, starting transfers between devices: none -> 69.5 us  [the longest x24 63.1 us: from_col(): return lax.ppermute(value, 'col', [(i ^ mask, i) for i in range(count)])]
    dot_general x3 -> x19, matrix products: 46.4 us -> 55.6 us  [product(): lax.dot_general(left, right, dims, preferred_element_type=jnp.float32)]
  transfers between devices with their start and end apart: 6 -> 38, of which waited for: 6 -> 17; matrix products, arithmetic and copies ran while one was open for 3% -> 20% of each run, Pallas kernels for 0% -> 0%
where the time goes in v2:
time: 317 us; the launch traced here: 314 us
  waiting for transfers between devices  164 us (52%)
  starting transfers between devices  69.5 us (22%)
  matrix products  55.6 us (18%)
  local copies, waits for them, and re-layouts  14.3 us (5%)
  other arithmetic  9.01 us (3%)
    ppermute x24, waiting for transfers between devices, from_col(): return lax.ppermute(value, 'col', [(i ^ mask, i) for i in range(count)])  95 us
    ppermute x14, waiting for transfers between devices, from_row(): return lax.ppermute(value, 'row', [(source(i), i) for i in range(count)])  68.9 us
    ppermute x24, starting transfers between devices, from_col(): return lax.ppermute(value, 'col', [(i ^ mask, i) for i in range(count)])  63.1 us
    dot_general x19, matrix products, product(): lax.dot_general(left, right, dims, preferred_element_type=jnp.float32)  55.6 us
    ppermute x14, starting transfers between devices, from_row(): return lax.ppermute(value, 'row', [(source(i), i) for i in range(count)])  6.39 us
  transfers between devices with their start and end apart: 38, of which 17 were waited for; matrix products, arithmetic and copies ran while one was open for 20% of the time, Pallas kernels for 0%

profile of v2, /device:TPU:0, one launch (start us, length us, event | category | flops | bytes accessed | tf_op | source)
XLA Modules:
  0.0 313.6 jit_solution(12253252908450675971)
XLA Ops:
  5.4 4.8 %convolution_convert_fusion.1 = bf16[544,1088]{1,0:T(8,128)(2,1)} fusion(bf16[1088,1024]{1,0:T(8,128)(2,1)} %param.1, s32[]{:T(128)S(6)} %select_n.179), kind=kOutput, calls=%fused_computation.5 | convolution fusion | flops 1212745728 | bytes 4526084 | tf_op jit(solution)/shard_map/own_sent/dot_general | solution.py:26
  16.3 3.3 %convolution_convert_fusion = bf16[544,1088]{1,0:T(8,128)(2,1)S(1)} fusion(bf16[1088,1024]{1,0:T(8,128)(2,1)} %collective-permute-done.2, bf16[1088,1024]{1,0:T(8,128)(2,1)S(1)} %copy-done, s32[]{:T(128)S(6)} %select_n.182), kind=kOutput, calls=%fused_computation.4 | convolution fusion | flops 1212745728 | bytes 4526084 | tf_op jit(solution)/shard_map/next_sent/dot_general | solution.py:26
  21.2 3.3 %fusion.10 = f32[544,1088]{1,0:T(8,128)S(1)} fusion(bf16[1088,1024]{1,0:T(8,128)(2,1)} %collective-permute-done.2, bf16[1088,1024]{1,0:T(8,128)(2,1)S(1)} %copy-done, s32[]{:T(128)S(6)} %select_n.183), kind=kOutput, calls=%fused_computation.31 | convolution fusion | flops 1212153856 | bytes 5709828 | tf_op jit(solution)/shard_map/next_kept/dot_general | solution.py:26
  24.5 5.1 %collective-permute-done.1 = bf16[512,1024]{1,0:T(8,128)(2,1)} collective-permute-done((bf16[512,1024]{1,0:T(8,128)(2,1)}, bf16[512,1024]{1,0:T(8,128)(2,1)}, u32[]{:S(2)}, u32[]{:S(2)}) %collective-permute-start.1) | collective-permute-done | bytes 1048608 | tf_op jit(solution)/shard_map/ppermute | solution.py:31
  35.7 4.2 %collective-permute-done = bf16[544,1088]{1,0:T(8,128)(2,1)S(1)} collective-permute-done((bf16[544,1088]{1,0:T(8,128)(2,1)}, bf16[544,1088]{1,0:T(8,128)(2,1)S(1)}, u32[]{:S(2)}, u32[]{:S(2)}) %collective-permute-start) | collective-permute-done | bytes 1183776 | tf_op jit(solution)/shard_map/ppermute | solution.py:36
  43.0 7.0 %collective-permute-done.6 = bf16[544,1088]{1,0:T(8,128)(2,1)S(1)} collective-permute-done((bf16[544,1088]{1,0:T(8,128)(2,1)S(1)}, bf16[544,1088]{1,0:T(8,128)(2,1)S(1)}, u32[]{:S(2)}, u32[]{:S(2)}) %collective-permute-start.6) | collective-permute-done | bytes 1183776 | tf_op jit(solution)/shard_map/ppermute | solution.py:36
  50.8 10.6 %collective-permute-done.5 = bf16[544,512]{1,0:T(8,128)(2,1)S(1)} collective-permute-done((bf16[544,512]{1,0:T(8,128)(2,1)S(1)}, bf16[544,512]{1,0:T(8,128)(2,1)S(1)}, u32[]{:S(2)}, u32[]{:S(2)}) %collective-permute-start.5) | collective-permute-done | bytes 557088 | tf_op jit(solution)/shard_map/ppermute | solution.py:36
  72.0 11.8 %collective-permute-done.8 = bf16[272,512]{1,0:T(8,128)(2,1)S(1)} collective-permute-done((bf16[272,512]{1,0:T(8,128)(2,1)S(1)}, bf16[272,512]{1,0:T(8,128)(2,1)S(1)}, u32[]{:S(2)}, u32[]{:S(2)}) %collective-permute-start.8) | collective-permute-done | bytes 278560 | tf_op jit(solution)/shard_map/ppermute | solution.py:36
  87.2 12.5 %collective-permute-done.9 = bf16[136,512]{1,0:T(8,128)(2,1)S(1)} collective-permute-done((bf16[136,512]{1,0:T(8,128)(2,1)S(1)}, bf16[136,512]{1,0:T(8,128)(2,1)S(1)}, u32[]{:S(2)}, u32[]{:S(2)}) %collective-permute-start.9) | collective-permute-done | bytes 139296 | tf_op jit(solution)/shard_map/ppermute | solution.py:36
  103.3 5.3 %collective-permute-start.18 = (bf16[272,576]{1,0:T(8,128)(2,1)S(1)}, bf16[272,576]{1,0:T(8,128)(2,1)S(1)}, u32[]{:S(2)}, u32[]{:S(2)}) collective-permute-start(bf16[272,576]{1,0:T(8,128)(2,1)S(1)} %dynamic-slice_convert_fusion.2), channel_id=1, source_target_pairs={{2,0},{3,1},{0,2},{1,3},{6,4},{7,5},{4,6},{5,7},{10,8},{11,9},{8,1... | collective-permute-start | bytes 940040 | tf_op jit(solution)/shard_map/ppermute | solution.py:36
  108.5 10.7 %collective-permute-done.13 = bf16[1,1,1,136,512]{4,3,2,1,0:T(8,128)(2,1)S(1)} collective-permute-done((bf16[1,1,1,136,512]{4,3,2,1,0:T(8,128)(2,1)S(1)}, bf16[1,1,1,136,512]{4,3,2,1,0:T(8,128)(2,1)S(1)}, u32[]{:S(2)}, u32[]{:S(2)}) %collective-permute-start.13) | collective-permute-done | bytes 139296 | tf_op jit(solution)/shard_map/ppermute | solution.py:36
  119.5 5.1 %collective-permute-done.11 = bf16[1,1,1,136,1088]{4,3,2,1,0:T(8,128)(2,1)S(1)} collective-permute-done((bf16[1,1,1,136,1088]{4,3,2,1,0:T(8,128)(2,1)S(1)}, bf16[1,1,1,136,1088]{4,3,2,1,0:T(8,128)(2,1)S(1)}, u32[]{:S(2)}, u32[]{:S(2)}) %collective-permute-start.11) | collective-permute-done | bytes 295968 | tf_op jit(solution)/shard_map/ppermute | solution.py:36
  126.8 3.8 %collective-permute-done.21 = bf16[1,1,2,136,512]{4,3,2,1,0:T(8,128)(2,1)S(1)} collective-permute-done((bf16[1,1,2,136,512]{4,3,2,1,0:T(8,128)(2,1)S(1)}, bf16[1,1,2,136,512]{4,3,2,1,0:T(8,128)(2,1)S(1)}, u32[]{:S(2)}, u32[]{:S(2)}) %collective-permute-start.21) | collective-permute-done | bytes 278560 | tf_op jit(solution)/shard_map/ppermute | solution.py:36
  130.6 8.0 %collective-permute-start.19 = (bf16[136,576]{1,0:T(8,128)(2,1)S(1)}, bf16[136,576]{1,0:T(8,128)(2,1)S(1)}, u32[]{:S(2)}, u32[]{:S(2)}) collective-permute-start(bf16[136,576]{1,0:T(8,128)(2,1)S(1)} %dynamic-slice_convert_fusion.6), channel_id=1, source_target_pairs={{4,0},{5,1},{6,2},{7,3},{0,4},{1,5},{2,6},{3,7},{12,8},{13,9},{14,... | collective-permute-start | bytes 470024 | tf_op jit(solution)/shard_map/ppermute | solution.py:36
  138.9 4.3 %collective-permute-done.19 = bf16[136,576]{1,0:T(8,128)(2,1)S(1)} collective-permute-done((bf16[136,576]{1,0:T(8,128)(2,1)S(1)}, bf16[136,576]{1,0:T(8,128)(2,1)S(1)}, u32[]{:S(2)}, u32[]{:S(2)}) %collective-permute-start.19) | collective-permute-done | bytes 156704 | tf_op jit(solution)/shard_map/ppermute | solution.py:36
  149.4 16.2 %collective-permute-done.23 = bf16[1,1,1,136,576]{4,3,2,1,0:T(8,128)(2,1)S(1)} collective-permute-done((bf16[1,1,1,136,576]{4,3,2,1,0:T(8,128)(2,1)S(1)}, bf16[1,1,1,136,576]{4,3,2,1,0:T(8,128)(2,1)S(1)}, u32[]{:S(2)}, u32[]{:S(2)}) %collective-permute-start.23) | collective-permute-done | bytes 156704 | tf_op jit(solution)/shard_map/ppermute | solution.py:36
  165.7 21.9 %collective-permute-start.24 = (bf16[1,1,2,136,576]{4,3,2,1,0:T(8,128)(2,1)S(1)}, bf16[1,1,2,136,576]{4,3,2,1,0:T(8,128)(2,1)S(1)}, u32[]{:S(2)}, u32[]{:S(2)}) collective-permute-start(bf16[1,1,2,136,576]{4,3,2,1,0:T(8,128)(2,1)S(1)} %constant_dynamic-update-slice_fusion.16), channel_id=1, source_target_pairs={{2,0},{3,1},{0,2},{1,3},{6,4},{7,5},{4,6},{5,7},{10,8},{11,9},{8,1... | collective-permute-start | bytes 940040 | tf_op jit(solution)/shard_map/ppermute | solution.py:36
  188.0 7.2 %collective-permute-done.24 = bf16[1,1,2,136,576]{4,3,2,1,0:T(8,128)(2,1)S(1)} collective-permute-done((bf16[1,1,2,136,576]{4,3,2,1,0:T(8,128)(2,1)S(1)}, bf16[1,1,2,136,576]{4,3,2,1,0:T(8,128)(2,1)S(1)}, u32[]{:S(2)}, u32[]{:S(2)}) %collective-permute-start.24) | collective-permute-done | bytes 313376 | tf_op jit(solution)/shard_map/ppermute | solution.py:36
  197.9 26.0 %collective-permute-done.30 = bf16[1,2,2,136,512]{4,3,2,1,0:T(8,128)(2,1)S(1)} collective-permute-done((bf16[1,2,2,136,512]{4,3,2,1,0:T(8,128)(2,1)S(1)}, bf16[1,2,2,136,512]{4,3,2,1,0:T(8,128)(2,1)S(1)}, u32[]{:S(2)}, u32[]{:S(2)}) %collective-permute-start.30) | collective-permute-done | bytes 557088 | tf_op jit(solution)/shard_map/ppermute | solution.py:31
  228.7 4.7 %fusion.27 = f32[1088,1024]{1,0:T(8,128)S(1)} fusion(bf16[1088,1088]{1,0:T(8,128)(2,1)S(1)} %bitcast.45, bf16[1088,1024]{1,0:T(8,128)(2,1)} %collective-permute-done.2), kind=kOutput, calls=%fused_computation.102 | convolution fusion | flops 2424307712 | bytes 9052160 | tf_op jit(solution)/shard_map/inner_next/dot_general | solution.py:26
  234.9 6.4 %collective-permute-done.32 = bf16[1,2,2,136,576]{4,3,2,1,0:T(8,128)(2,1)S(1)} collective-permute-done((bf16[1,2,2,136,576]{4,3,2,1,0:T(8,128)(2,1)S(1)}, bf16[1,2,2,136,576]{4,3,2,1,0:T(8,128)(2,1)S(1)}, u32[]{:S(2)}, u32[]{:S(2)}) %collective-permute-start.32) | collective-permute-done | bytes 626720 | tf_op jit(solution)/shard_map/ppermute | solution.py:31
  255.1 25.1 %collective-permute-done.33 = bf16[544,1024]{1,0:T(8,128)(2,1)} collective-permute-done((bf16[544,1024]{1,0:T(8,128)(2,1)S(1)}, bf16[544,1024]{1,0:T(8,128)(2,1)}, u32[]{:S(2)}, u32[]{:S(2)}) %collective-permute-start.33) | collective-permute-done | bytes 1114144 | tf_op jit(solution)/shard_map/ppermute | solution.py:31
  297.4 6.3 %collective-permute-done.36 = bf16[544,1024]{1,0:T(8,128)(2,1)} collective-permute-done((bf16[544,1024]{1,0:T(8,128)(2,1)S(1)}, bf16[544,1024]{1,0:T(8,128)(2,1)}, u32[]{:S(2)}, u32[]{:S(2)}) %collective-permute-start.36) | collective-permute-done | bytes 1114144 | tf_op jit(solution)/shard_map/ppermute | solution.py:31
  305.3 3.4 %convolution_add_fusion = f32[1088,1024]{1,0:T(8,128)S(1)} fusion(f32[1088,1024]{1,0:T(8,128)S(1)} %add.243, bf16[1088,1088]{1,0:T(8,128)(2,1)S(1)} %constant_dynamic-update-slice_fusion.1, bf16[1088,1024]{1,0:T(8,128)(2,1)S(1)} %constant_dynamic-update-slice_fusion.5), kind=kOutput, calls=%fused_computation | convolution fusion | flops 2425421824 | bytes 13508608 | tf_op jit(solution)/shard_map/outer_far_other/dot_general | solution.py:26
  (168 shorter events, 95.5 us)
Async XLA Ops:
  2.8 26.8 %collective-permute-start.1 = (bf16[512,1024]{1,0:T(8,128)(2,1)}, bf16[512,1024]{1,0:T(8,128)(2,1)}, u32[]{:S(2)}, u32[]{:S(2)}) collective-permute-start(bf16[512,1024]{1,0:T(8,128)(2,1)} %slice.6), channel_id=1, source_target_pairs={{16,0},{24,8},{8,16},{0,24},{17,1},{25,9},{9,17},{1,25},{18,2},{26... | collective-permute-start | bytes 3145736 | tf_op jit(solution)/shard_map/ppermute | solution.py:31
  10.2 29.7 %collective-permute-start = (bf16[544,1088]{1,0:T(8,128)(2,1)}, bf16[544,1088]{1,0:T(8,128)(2,1)S(1)}, u32[]{:S(2)}, u32[]{:S(2)}) collective-permute-start(bf16[544,1088]{1,0:T(8,128)(2,1)} %convolution_convert_fusion.1), channel_id=1, source_target_pairs={{2,0},{3,1},{0,2},{1,3},{6,4},{7,5},{4,6},{5,7},{10,8},{11,9},{8,1... | collective-permute-start | bytes 3551240 | tf_op jit(solution)/shard_map/ppermute | solution.py:36
  16.0 46.0 %collective-permute-start.4 = (bf16[576,1024]{1,0:T(8,128)(2,1)}, bf16[576,1024]{1,0:T(8,128)(2,1)}, u32[]{:S(2)}, u32[]{:S(2)}) collective-permute-start(bf16[576,1024]{1,0:T(8,128)(2,1)} %slice.7), channel_id=1, source_target_pairs={{16,0},{24,8},{8,16},{0,24},{17,1},{25,9},{9,17},{1,25},{18,2},{26... | collective-permute-start | bytes 3538952 | tf_op jit(solution)/shard_map/ppermute | solution.py:31
  19.6 30.4 %collective-permute-start.6 = (bf16[544,1088]{1,0:T(8,128)(2,1)S(1)}, bf16[544,1088]{1,0:T(8,128)(2,1)S(1)}, u32[]{:S(2)}, u32[]{:S(2)}) collective-permute-start(bf16[544,1088]{1,0:T(8,128)(2,1)S(1)} %convolution_convert_fusion), channel_id=1, source_target_pairs={{1,0},{0,1},{3,2},{2,3},{5,4},{4,5},{7,6},{6,7},{9,8},{8,9},{11,10... | collective-permute-start | bytes 3551240 | tf_op jit(solution)/shard_map/ppermute | solution.py:36
  31.6 29.8 %collective-permute-start.5 = (bf16[544,512]{1,0:T(8,128)(2,1)S(1)}, bf16[544,512]{1,0:T(8,128)(2,1)S(1)}, u32[]{:S(2)}, u32[]{:S(2)}) collective-permute-start(bf16[544,512]{1,0:T(8,128)(2,1)S(1)} %convolution_convert_fusion.3), channel_id=1, source_target_pairs={{1,0},{0,1},{3,2},{2,3},{5,4},{4,5},{7,6},{6,7},{9,8},{8,9},{11,10... | collective-permute-start | bytes 1671176 | tf_op jit(solution)/shard_map/ppermute | solution.py:36
  40.3 29.8 %collective-permute-start.3 = (bf16[272,1088]{1,0:T(8,128)(2,1)S(1)}, bf16[272,1088]{1,0:T(8,128)(2,1)S(1)}, u32[]{:S(2)}, u32[]{:S(2)}) collective-permute-start(bf16[272,1088]{1,0:T(8,128)(2,1)S(1)} %dynamic-slice_convert_fusion.1), channel_id=1, source_target_pairs={{4,0},{5,1},{6,2},{7,3},{0,4},{1,5},{2,6},{3,7},{12,8},{13,9},{14,... | collective-permute-start | bytes 1775624 | tf_op jit(solution)/shard_map/ppermute | solution.py:36
  50.3 35.3 %collective-permute-start.10 = (bf16[272,1088]{1,0:T(8,128)(2,1)S(1)}, bf16[272,1088]{1,0:T(8,128)(2,1)S(1)}, u32[]{:S(2)}, u32[]{:S(2)}) collective-permute-start(bf16[272,1088]{1,0:T(8,128)(2,1)S(1)} %dynamic-slice_convert_fusion), channel_id=1, source_target_pairs={{2,0},{3,1},{0,2},{1,3},{6,4},{7,5},{4,6},{5,7},{10,8},{11,9},{8,1... | collective-permute-start | bytes 1775624 | tf_op jit(solution)/shard_map/ppermute | solution.py:36
  64.3 38.7 %collective-permute-start.14 = (bf16[544,576]{1,0:T(8,128)(2,1)S(1)}, bf16[544,576]{1,0:T(8,128)(2,1)S(1)}, u32[]{:S(2)}, u32[]{:S(2)}) collective-permute-start(bf16[544,576]{1,0:T(8,128)(2,1)S(1)} %convolution_convert_fusion.2), channel_id=1, source_target_pairs={{1,0},{0,1},{3,2},{2,3},{5,4},{4,5},{7,6},{6,7},{9,8},{8,9},{11,10... | collective-permute-start | bytes 1880072 | tf_op jit(solution)/shard_map/ppermute | solution.py:36
  70.3 29.4 %collective-permute-start.7 = (bf16[136,1088]{1,0:T(8,128)(2,1)S(1)}, bf16[136,1088]{1,0:T(8,128)(2,1)S(1)}, u32[]{:S(2)}, u32[]{:S(2)}) collective-permute-start(bf16[136,1088]{1,0:T(8,128)(2,1)S(1)} %dynamic-slice_convert_fusion.4), channel_id=1, source_target_pairs={{1,0},{0,1},{3,2},{2,3},{5,4},{4,5},{7,6},{6,7},{9,8},{8,9},{11,10... | collective-permute-start | bytes 887816 | tf_op jit(solution)/shard_map/ppermute | solution.py:36
  85.8 33.6 %collective-permute-start.12 = (bf16[136,1088]{1,0:T(8,128)(2,1)S(1)}, bf16[136,1088]{1,0:T(8,128)(2,1)S(1)}, u32[]{:S(2)}, u32[]{:S(2)}) collective-permute-start(bf16[136,1088]{1,0:T(8,128)(2,1)S(1)} %dynamic-slice_convert_fusion.3), channel_id=1, source_target_pairs={{4,0},{5,1},{6,2},{7,3},{0,4},{1,5},{2,6},{3,7},{12,8},{13,9},{14,... | collective-permute-start | bytes 887816 | tf_op jit(solution)/shard_map/ppermute | solution.py:36
  99.9 24.7 %collective-permute-start.11 = (bf16[1,1,1,136,1088]{4,3,2,1,0:T(8,128)(2,1)S(1)}, bf16[1,1,1,136,1088]{4,3,2,1,0:T(8,128)(2,1)S(1)}, u32[]{:S(2)}, u32[]{:S(2)}) collective-permute-start(bf16[1,1,1,136,1088]{4,3,2,1,0:T(8,128)(2,1)S(1)} %bitcast.50), channel_id=1, source_target_pairs={{4,0},{5,1},{6,2},{7,3},{0,4},{1,5},{2,6},{3,7},{12,8},{13,9},{14,... | collective-permute-start | bytes 887816 | tf_op jit(solution)/shard_map/ppermute | solution.py:36
  103.3 23.2 %collective-permute-start.18 = (bf16[272,576]{1,0:T(8,128)(2,1)S(1)}, bf16[272,576]{1,0:T(8,128)(2,1)S(1)}, u32[]{:S(2)}, u32[]{:S(2)}) collective-permute-start(bf16[272,576]{1,0:T(8,128)(2,1)S(1)} %dynamic-slice_convert_fusion.2), channel_id=1, source_target_pairs={{2,0},{3,1},{0,2},{1,3},{6,4},{7,5},{4,6},{5,7},{10,8},{11,9},{8,1... | collective-permute-start | bytes 940040 | tf_op jit(solution)/shard_map/ppermute | solution.py:36
  138.7 49.0 %collective-permute-start.27 = (bf16[1,2,2,136,512]{4,3,2,1,0:T(8,128)(2,1)S(1)}, bf16[1,2,2,136,512]{4,3,2,1,0:T(8,128)(2,1)S(1)}, u32[]{:S(2)}, u32[]{:S(2)}) collective-permute-start(bf16[1,2,2,136,512]{4,3,2,1,0:T(8,128)(2,1)S(1)} %constant_dynamic-update-slice_fusion.22), channel_id=1, source_target_pairs={{24,0},{16,8},{0,16},{8,24},{25,1},{17,9},{1,17},{9,25},{26,2},{18... | collective-permute-start | bytes 1671176 | tf_op jit(solution)/shard_map/ppermute | solution.py:31
  143.2 44.5 %collective-permute-start.26 = (bf16[1,2,2,136,512]{4,3,2,1,0:T(8,128)(2,1)S(1)}, bf16[1,2,2,136,512]{4,3,2,1,0:T(8,128)(2,1)S(1)}, u32[]{:S(2)}, u32[]{:S(2)}) collective-permute-start(bf16[1,2,2,136,512]{4,3,2,1,0:T(8,128)(2,1)S(1)} %constant_dynamic-update-slice_fusion.22), channel_id=1, source_target_pairs={{1,0},{0,1},{3,2},{2,3},{5,4},{4,5},{7,6},{6,7},{9,8},{8,9},{11,10... | collective-permute-start | bytes 1671176 | tf_op jit(solution)/shard_map/ppermute | solution.py:36
  144.7 42.9 %collective-permute-start.25 = (bf16[2,1,1,136,1088]{4,3,2,1,0:T(8,128)(2,1)S(1)}, bf16[2,1,1,136,1088]{4,3,2,1,0:T(8,128)(2,1)S(1)}, u32[]{:S(2)}, u32[]{:S(2)}) collective-permute-start(bf16[2,1,1,136,1088]{4,3,2,1,0:T(8,128)(2,1)S(1)} %constant_dynamic-update-slice_fusion.20), channel_id=1, source_target_pairs={{4,0},{5,1},{6,2},{7,3},{0,4},{1,5},{2,6},{3,7},{12,8},{13,9},{14,... | collective-permute-start | bytes 1775624 | tf_op jit(solution)/shard_map/ppermute | solution.py:36
  148.0 76.4 %collective-permute-start.22 = (bf16[2,2,1,136,1088]{4,3,2,1,0:T(8,128)(2,1)S(1)}, bf16[2,2,1,136,1088]{4,3,2,1,0:T(8,128)(2,1)S(1)}, u32[]{:S(2)}, u32[]{:S(2)}) collective-permute-start(bf16[2,2,1,136,1088]{4,3,2,1,0:T(8,128)(2,1)S(1)} %constant_dynamic-update-slice_fusion.18), channel_id=1, source_target_pairs={{1,0},{0,1},{3,2},{2,3},{5,4},{4,5},{7,6},{6,7},{9,8},{8,9},{11,10... | collective-permute-start | bytes 3551240 | tf_op jit(solution)/shard_map/ppermute | solution.py:36
  165.7 29.4 %collective-permute-start.24 = (bf16[1,1,2,136,576]{4,3,2,1,0:T(8,128)(2,1)S(1)}, bf16[1,1,2,136,576]{4,3,2,1,0:T(8,128)(2,1)S(1)}, u32[]{:S(2)}, u32[]{:S(2)}) collective-permute-start(bf16[1,1,2,136,576]{4,3,2,1,0:T(8,128)(2,1)S(1)} %constant_dynamic-update-slice_fusion.16), channel_id=1, source_target_pairs={{2,0},{3,1},{0,2},{1,3},{6,4},{7,5},{4,6},{5,7},{10,8},{11,9},{8,1... | collective-permute-start | bytes 940040 | tf_op jit(solution)/shard_map/ppermute | solution.py:36
  195.3 28.6 %collective-permute-start.29 = (bf16[1,2,2,136,576]{4,3,2,1,0:T(8,128)(2,1)S(1)}, bf16[1,2,2,136,576]{4,3,2,1,0:T(8,128)(2,1)S(1)}, u32[]{:S(2)}, u32[]{:S(2)}) collective-permute-start(bf16[1,2,2,136,576]{4,3,2,1,0:T(8,128)(2,1)S(1)} %constant_dynamic-update-slice_fusion.12), channel_id=1, source_target_pairs={{24,0},{16,8},{0,16},{8,24},{25,1},{17,9},{1,17},{9,25},{26,2},{18... | collective-permute-start | bytes 1880072 | tf_op jit(solution)/shard_map/ppermute | solution.py:31
  195.4 28.6 %collective-permute-start.28 = (bf16[1,2,2,136,576]{4,3,2,1,0:T(8,128)(2,1)S(1)}, bf16[1,2,2,136,576]{4,3,2,1,0:T(8,128)(2,1)S(1)}, u32[]{:S(2)}, u32[]{:S(2)}) collective-permute-start(bf16[1,2,2,136,576]{4,3,2,1,0:T(8,128)(2,1)S(1)} %constant_dynamic-update-slice_fusion.12), channel_id=1, source_target_pairs={{1,0},{0,1},{3,2},{2,3},{5,4},{4,5},{7,6},{6,7},{9,8},{8,9},{11,10... | collective-permute-start | bytes 1880072 | tf_op jit(solution)/shard_map/ppermute | solution.py:36
  196.1 27.9 %collective-permute-start.30 = (bf16[1,2,2,136,512]{4,3,2,1,0:T(8,128)(2,1)S(1)}, bf16[1,2,2,136,512]{4,3,2,1,0:T(8,128)(2,1)S(1)}, u32[]{:S(2)}, u32[]{:S(2)}) collective-permute-start(bf16[1,2,2,136,512]{4,3,2,1,0:T(8,128)(2,1)S(1)} %collective-permute-done.26), channel_id=1, source_target_pairs={{24,0},{16,8},{0,16},{8,24},{25,1},{17,9},{1,17},{9,25},{26,2},{18... | collective-permute-start | bytes 1671176 | tf_op jit(solution)/shard_map/ppermute | solution.py:31
  196.5 31.6 %collective-permute-start.31 = (bf16[2,1,2,136,1088]{4,3,2,1,0:T(8,128)(2,1)S(1)}, bf16[2,1,2,136,1088]{4,3,2,1,0:T(8,128)(2,1)S(1)}, u32[]{:S(2)}, u32[]{:S(2)}) collective-permute-start(bf16[2,1,2,136,1088]{4,3,2,1,0:T(8,128)(2,1)S(1)} %constant_dynamic-update-slice_fusion.14), channel_id=1, source_target_pairs={{2,0},{3,1},{0,2},{1,3},{6,4},{7,5},{4,6},{5,7},{10,8},{11,9},{8,1... | collective-permute-start | bytes 3551240 | tf_op jit(solution)/shard_map/ppermute | solution.py:36
  252.6 30.7 %collective-permute-start.34 = (bf16[1088,1024]{1,0:T(8,128)(2,1)S(1)}, bf16[1088,1024]{1,0:T(8,128)(2,1)S(1)}, u32[]{:S(2)}, u32[]{:S(2)}) collective-permute-start(bf16[1088,1024]{1,0:T(8,128)(2,1)S(1)} %constant_dynamic-update-slice_fusion.3), channel_id=1, source_target_pairs={{8,0},{0,8},{24,16},{16,24},{9,1},{1,9},{25,17},{17,25},{10,2},{2,... | collective-permute-start | bytes 6684680 | tf_op jit(solution)/shard_map/ppermute | solution.py:31
  252.7 27.5 %collective-permute-start.33 = (bf16[544,1024]{1,0:T(8,128)(2,1)S(1)}, bf16[544,1024]{1,0:T(8,128)(2,1)}, u32[]{:S(2)}, u32[]{:S(2)}) collective-permute-start(bf16[544,1024]{1,0:T(8,128)(2,1)S(1)} %add_convert_fusion.1), channel_id=1, source_target_pairs={{16,0},{24,8},{8,16},{0,24},{17,1},{25,9},{9,17},{1,25},{18,2},{26... | collective-permute-start | bytes 3342344 | tf_op jit(solution)/shard_map/ppermute | solution.py:31
  253.1 50.6 %collective-permute-start.36 = (bf16[544,1024]{1,0:T(8,128)(2,1)S(1)}, bf16[544,1024]{1,0:T(8,128)(2,1)}, u32[]{:S(2)}, u32[]{:S(2)}) collective-permute-start(bf16[544,1024]{1,0:T(8,128)(2,1)S(1)} %add_convert_fusion), channel_id=1, source_target_pairs={{16,0},{24,8},{8,16},{0,24},{17,1},{25,9},{9,17},{1,25},{18,2},{26... | collective-permute-start | bytes 3342344 | tf_op jit(solution)/shard_map/ppermute | solution.py:31
  (20 other events, 255.8 us)
